TPU v7x, 1024 devices: a whole 4x4x32 slice. The times are simulated.
1024 devices in a mesh: dom: 128 (over z, y), grp: 8 (over x, core).
Axes of the slice: x: 4, y: 4, z: 32, core: 2. Of those that a mesh axis runs over, the one named last changes fastest.
Arguments:
- features: bfloat16 [1048576, 256], P(('dom', 'grp')), may hold values from -6 to 6
- cotangent: bfloat16 [1048576, 256], P(('dom', 'grp')), may hold values from -6 to 6
- w_self: bfloat16 [256, 256], replicated, may hold values from -0.375 to 0.375
- w_nbr: bfloat16 [256, 256], replicated, may hold values from -0.375 to 0.375
- tile_vals: bfloat16 [1024, 40, 128, 128], P(('dom', 'grp')), may hold values from 0 to 0.2, as said below
- tile_dst: int32 [1024, 40], P(('dom', 'grp')), may hold values from 0 to 7, as said below
- tile_src: int32 [1024, 40], P(('dom', 'grp')), may hold values from 0 to 10, as said below
- tile_count: int32 [1024], P(('dom', 'grp')), may hold values from 10 to 40, as said below
- send_rows: int32 [1024, 256], P(('dom', 'grp')), may hold values from 0 to 1023
- hub_rows: int32 [1024, 16], P(('dom', 'grp')), may hold values from 0 to 1023, as said below
Outputs:
- activations: bfloat16 [1048576, 256], P(('dom', 'grp'))
- grad_features: bfloat16 [1048576, 256], P(('dom', 'grp'))
- grad_w_self: float32 [256, 256], replicated
- grad_w_nbr: float32 [256, 256], replicated
Inputs may be any that keep to these rules, and one draw needn't show every extreme that they name: `tile_vals`: edge weights; slots from tile_count on are padding with stale values. A device's tiles name distinct pairs of tile_dst and tile_src. `tile_src`: blocks 0 to 7 are own rows, the next 2 boundary rows, the last 1 hub copies. `tile_count`: some device has all 40 slots live in every draw. `send_rows`: entries p * 2 to (p + 1) * 2 - 1 go to dom peer p; rows may repeat. `hub_rows`: distinct on each device.
All inputs are finite; a program needn't handle non-finite values.
Results may differ from a plain program's by a relative error of at most 0.0053.
Values may be sent and summed in bfloat16 or wider, within the bound.
No kernel may reach another device: no remote copies, remote signals or barrier semaphores. Data moves between devices by JAX's collectives and lax.ppermute only.
A program may use at most 64 MiB of HBM per device.

v0:
```python
import math

import jax
import jax.numpy as jnp
from jax import lax
from jax.sharding import PartitionSpec as P


def per_device(
    features,
    cotangent,
    w_self,
    w_nbr,
    tile_vals,
    tile_dst,
    tile_src,
    tile_count,
    send_rows,
    hub_rows,
):
    node_rows = features.shape[0]
    width = features.shape[1]
    tile_total = tile_vals.shape[1]
    tile_size = tile_vals.shape[2]
    sent_rows = features[send_rows[0]]
    boundary = lax.all_to_all(sent_rows, "dom", split_axis=0, concat_axis=0, tiled=True)
    hub_copies = lax.all_gather(features[hub_rows[0]], "grp", axis=0, tiled=True)
    source = jnp.concatenate([features, boundary, hub_copies], axis=0)
    block_count = source.shape[0] // tile_size
    local_count = node_rows // tile_size
    source_blocks = source.reshape(block_count, tile_size, width)
    tile_block = tile_vals[0]
    dst_ids = tile_dst[0]
    src_ids = tile_src[0]
    live_mask = (jnp.arange(tile_total, dtype=jnp.int32) < tile_count[0]).astype(jnp.float32)
    gathered = source_blocks[src_ids]
    products = jnp.einsum("tij,tjd->tid", tile_block, gathered, preferred_element_type=jnp.float32)
    dst_onehot = (dst_ids[:, None] == jnp.arange(local_count, dtype=jnp.int32)[None, :]).astype(
        jnp.float32
    ) * live_mask[:, None]
    aggregated = jnp.einsum("tb,tid->bid", dst_onehot, products, precision=lax.Precision.HIGHEST)
    aggregated = aggregated.reshape(node_rows, width).astype(jnp.bfloat16)
    pre = jnp.dot(features, w_self, preferred_element_type=jnp.float32) + jnp.dot(
        aggregated, w_nbr, preferred_element_type=jnp.float32
    )
    sigmoid_pre = jax.nn.sigmoid(pre)
    activations = (pre * sigmoid_pre).astype(jnp.bfloat16)
    pre_grad = (
        cotangent.astype(jnp.float32) * sigmoid_pre * (1.0 + pre * (1.0 - sigmoid_pre))
    ).astype(jnp.bfloat16)
    contract_last = (((1,), (1,)), ((), ()))
    self_grad = lax.dot_general(pre_grad, w_self, contract_last, preferred_element_type=jnp.float32)
    agg_grad = lax.dot_general(
        pre_grad, w_nbr, contract_last, preferred_element_type=jnp.float32
    ).astype(jnp.bfloat16)
    picked = agg_grad.reshape(local_count, tile_size, width)[dst_ids]
    pieces = jnp.einsum("tij,tid->tjd", tile_block, picked, preferred_element_type=jnp.float32)
    src_onehot = (src_ids[:, None] == jnp.arange(block_count, dtype=jnp.int32)[None, :]).astype(
        jnp.float32
    ) * live_mask[:, None]
    source_grad = jnp.einsum("ts,tjd->sjd", src_onehot, pieces, precision=lax.Precision.HIGHEST)
    source_grad = source_grad.reshape(block_count * tile_size, width)
    halo_end = node_rows + boundary.shape[0]
    boundary_grad = source_grad[node_rows:halo_end].astype(jnp.bfloat16)
    hub_part = source_grad[halo_end:]
    returned = lax.all_to_all(boundary_grad, "dom", split_axis=0, concat_axis=0, tiled=True)
    device_total = node_rows * lax.axis_size("dom") * lax.axis_size("grp")
    grad_scale = 1.0 / math.sqrt(device_total)
    contract_rows = (((0,), (0,)), ((), ()))
    self_term = (
        lax.dot_general(features, pre_grad, contract_rows, preferred_element_type=jnp.float32)
        * grad_scale
    )
    nbr_term = (
        lax.dot_general(aggregated, pre_grad, contract_rows, preferred_element_type=jnp.float32)
        * grad_scale
    )
    hub_sums = lax.psum_scatter(
        hub_part.astype(jnp.bfloat16), "grp", scatter_dimension=0, tiled=True
    ).astype(jnp.float32)
    grad_w_self, grad_w_nbr = lax.psum((self_term, nbr_term), ("dom", "grp"))
    summed = self_grad + source_grad[:node_rows]
    summed = summed.at[send_rows[0]].add(returned.astype(jnp.float32))
    summed = summed.at[hub_rows[0]].add(hub_sums)
    return (activations, summed.astype(jnp.bfloat16), grad_w_self, grad_w_nbr)


def solution(mesh):
    return jax.shard_map(
        per_device,
        mesh=mesh,
        in_specs=(
            P(("dom", "grp"), None),
            P(("dom", "grp"), None),
            P(),
            P(),
            P(("dom", "grp"), None, None, None),
            P(("dom", "grp"), None),
            P(("dom", "grp"), None),
            P(("dom", "grp")),
            P(("dom", "grp"), None),
            P(("dom", "grp"), None),
        ),
        out_specs=(P(("dom", "grp"), None), P(("dom", "grp"), None), P(), P()),
        check_vma=False,
    )
```

profile of v0, /device:TPU:1, one launch (start us, length us, event | category | flops | bytes accessed | tf_op | source)
XLA Modules:
  0.0 1042.5 jit_solution(15750563925735757609)
XLA Ops:
  8.0 0.0 copy-start
  8.0 0.0 copy-start.1
  8.0 0.8 compare_select_fusion
  8.8 2.1 gather_fusion
  10.9 0.7 all_to_all.12
  11.6 33.8 %all-to-all-start = ((bf16[128,2,256]{2,1,0:T(2,128)(2,1)}), bf16[128,2,256]{2,1,0:T(2,128)(2,1)S(1)}, u32[]{:S(2)}, u32[]{:S(2)}) async-start(bf16[128,2,256]{2,1,0:T(2,128)(2,1)} %all_to_all.12), calls=%async_computation | async-start | bytes 262144 | tf_op jit(solution)/shard_map/all_to_all | solution.py:26
  46.0 0.7 fusion.24
  46.7 1.7 gather_fusion.1
  48.4 14.0 %all-gather = bf16[128,256]{1,0:T(8,128)(2,1)S(1)} all-gather(bf16[16,256]{1,0:T(8,128)(2,1)S(1)} %gather_fusion.1), channel_id=2, replica_groups=mesh['dom'=128,'grp'=8] {'grp'}, dimensions={0}, use_global_device_ids=true | all-gather | bytes 73728 | tf_op jit(solution)/shard_map/all_gather | solution.py:27
  62.4 0.7 fusion.25
  63.1 0.7 fusion.26
  63.8 2.4 fusion.29
  66.1 4.7 all-to-all-done
  70.8 0.1 all_to_all.14
  70.9 2.4 gather_fusion.2
  73.3 4.9 fusion.6
  78.2 6.2 copy.21
  84.4 0.0 copy-start.10
  84.4 5.3 fusion.8
  89.8 0.1 copy.17
  89.9 1.5 multiply_convert_fusion
  91.4 0.8 copy-done.2
  92.2 0.3 convolution_convert_fusion
  92.5 2.4 gather_fusion.3
  94.9 4.9 fusion.4
  99.8 6.2 copy.22
  106.0 4.6 fusion
  110.7 0.8 copy.24
  111.5 0.9 copy-done.3
  112.3 0.7 convert_element_type.55
  113.1 20.8 %all-to-all-start.1 = ((bf16[128,2,256]{2,1,0:T(2,128)(2,1)}), bf16[128,2,256]{2,1,0:T(2,128)(2,1)S(1)}, u32[]{:S(2)}, u32[]{:S(2)}) async-start(bf16[128,2,256]{2,1,0:T(2,128)(2,1)} %convert_element_type.55), calls=%async_computation.1 | async-start | bytes 262144 | tf_op jit(solution)/shard_map/all_to_all | solution.py:66
  133.8 0.0 all-reduce.3.cloned.1.call-start
  133.9 2.2 convolution_multiply_fusion
  136.1 2.2 fusion.11
  138.3 0.0 all-reduce.3.cloned.1.call-update
  138.4 0.0 reduce-scatter.2.cloned.1.call-start
  138.4 0.1 slice.28
  138.5 0.3 copy.18
  138.9 1.5 slice_bitcast_fusion
  140.3 0.0 reduce-scatter.2.cloned.1.call-update
  140.4 1.4 convolution_add_fusion
  141.8 886.2 %all-reduce.3.cloned.1.call-done = (f32[256,256]{0,1:T(8,128)}, f32[256,256]{1,0:T(8,128)}) async-done(((f32[256,256]{0,1:T(8,128)}, f32[256,256]{1,0:T(8,128)}), (f32[256,256]{0,1:T(8,128)}, f32[256,256]{1,0:T(8,128)})) %all-reduce.3.cloned.1.call-update) | async-done | bytes 524304 | tf_op jit(solution)/shard_map/psum | solution.py:81
  1028.0 1.8 copy.20
  1029.9 2.4 scatter_fusion
  1032.2 0.0 reduce-scatter.2.cloned.1.call-done
  1032.3 1.3 scatter_custom_fusion.1
  1033.5 0.8 convert_element_type.60
  1034.4 0.7 copy.30
  (26 shorter events, 0.2 us)
Async XLA Ops:
  8.0 65.3 %copy-start = (bf16[1,40,128,128]{3,2,1,0:T(8,128)(2,1)S(1)}, bf16[1,40,128,128]{3,2,1,0:T(8,128)(2,1)}, u32[]{:S(2)}) copy-start(bf16[1,40,128,128]{3,2,1,0:T(8,128)(2,1)} %param.14) | copy-start | bytes 3932164
  8.0 62.9 %copy-start.1 = (bf16[1024,256]{1,0:T(8,128)(2,1)S(1)}, bf16[1024,256]{1,0:T(8,128)(2,1)}, u32[]{:S(2)}) copy-start(bf16[1024,256]{1,0:T(8,128)(2,1)} %param.10) | copy-start | bytes 1572868
  11.6 59.2 %all-to-all-start = ((bf16[128,2,256]{2,1,0:T(2,128)(2,1)}), bf16[128,2,256]{2,1,0:T(2,128)(2,1)S(1)}, u32[]{:S(2)}, u32[]{:S(2)}) async-start(bf16[128,2,256]{2,1,0:T(2,128)(2,1)} %all_to_all.12), calls=%async_computation | async-start | bytes 262144 | tf_op jit(solution)/shard_map/all_to_all | solution.py:26
  78.2 6.2 copy-start.8
  84.4 5.5 copy-start.4
  84.4 5.5 copy-start.7
  84.4 5.5 copy-start.10
  89.9 1.5 copy-start.5
  91.4 0.8 copy-start.2
  99.8 6.2 copy-start.9
  111.4 0.9 copy-start.3
  113.1 916.7 %all-to-all-start.1 = ((bf16[128,2,256]{2,1,0:T(2,128)(2,1)}), bf16[128,2,256]{2,1,0:T(2,128)(2,1)S(1)}, u32[]{:S(2)}, u32[]{:S(2)}) async-start(bf16[128,2,256]{2,1,0:T(2,128)(2,1)} %convert_element_type.55), calls=%async_computation.1 | async-start | bytes 262144 | tf_op jit(solution)/shard_map/all_to_all | solution.py:66
  133.8 894.2 %all-reduce.3.cloned.1.call-start = ((), (), s32[]{:S(2)}) async-start(), calls=%async_computation.4 | async-start | bytes 1048576 | tf_op jit(solution)/shard_map/psum | solution.py:81
  138.4 893.9 %reduce-scatter.2.cloned.1.call-start = ((), (), s32[]{:S(2)}) async-start(), calls=%async_computation.3 | async-start | bytes 73728 | tf_op jit(solution)/shard_map/reduce_scatter | solution.py:78
  1029.8 4.5 copy-start.6
Sparse Core Ops, SparseCore 0:
  141.6 886.3 all-reduce.2
Sparse Core Ops, SparseCore 1:
  142.2 47.7 reduce-scatter.1
where the time goes:
time: 1040 us
  waiting for transfers between devices  891 us (86%)
  starting transfers between devices  54.6 us (5%)
  matrix products  29.9 us (3%)
  local copies, waits for them, and re-layouts  29.4 us (3%)
  between operations  16.3 us (2%)
  blocking collectives  14 us (1%)
    psum x1, waiting for transfers between devices, per_device(): grad_w_self, grad_w_nbr = lax.psum((self_term, nbr_term), ('dom', 'grp'))  886 us
    all_to_all x1, starting transfers between devices, per_device(): lax.all_to_all(sent_rows, 'dom', split_axis=0, concat_axis=0, tiled=True)  33.8 us
  transfers between devices with their start and end apart: 4, of which 2 were waited for; matrix products, arithmetic and copies ran while one was open for 2% of the time, Pallas kernels for 0%

commit v1 on v0

v1 whole, which is shorter than its diff:
```python
import math

import jax
import jax.numpy as jnp
from jax import lax
from jax.experimental import pallas as pl
from jax.experimental.pallas import tpu as pltpu
from jax.sharding import Mesh
from jax.sharding import PartitionSpec as P

TILE = 128
ROWS = 1024
HALO = 256
HUBS = 128
HUB_DEV = 16
PART = 64
LOAD = PART + HUB_DEV
LOCAL = 8
SOURCE = 11
TILES = 40
D = 256
CHUNK = 256
AXES = ("zh", "zl", "y", "x", "c")
ZL = 8
ZH = 4
BF16 = jnp.bfloat16
F32 = jnp.float32
VMEM_LIMIT = 60 * 1024 * 1024
SMALL_LIMIT = 16 * 1024 * 1024

VM = pl.BlockSpec(memory_space=pltpu.VMEM)
ANY = pl.BlockSpec(memory_space=pl.ANY)
SM = pl.BlockSpec(memory_space=pltpu.SMEM)


def dot(a, b):
    return jnp.dot(a, b, preferred_element_type=F32)


def call(kernel, outs, specs, scratch=(), flops=0, nbytes=0, trans=0, limit=VMEM_LIMIT):
    return pl.pallas_call(
        kernel,
        out_shape=[jax.ShapeDtypeStruct(s, t) for s, t in outs],
        in_specs=list(specs),
        out_specs=[VM] * len(outs),
        scratch_shapes=list(scratch),
        compiler_params=pltpu.CompilerParams(vmem_limit_bytes=limit),
        cost_estimate=pl.CostEstimate(flops=flops, bytes_accessed=nbytes, transcendentals=trans),
    )


def column_of(row, count):
    here = lax.broadcasted_iota(jnp.int32, (count, count), 0)
    there = lax.broadcasted_iota(jnp.int32, (count, count), 1)
    spread = jnp.where(here == there, jnp.broadcast_to(row, (count, count)).astype(F32), 0.0)
    return jnp.sum(spread, axis=1, keepdims=True).astype(jnp.int32)


def pick_kernel(send_ref, hub_ref, x_ref, sent_ref, hubs_ref):
    for idx_ref, out_ref in ((hub_ref, hubs_ref), (send_ref, sent_ref)):
        count = out_ref.shape[0]
        column = column_of(idx_ref[...], count)
        lanes = lax.broadcasted_iota(jnp.int32, (count, ROWS), 1)
        onehot = jnp.where(lanes == column, 1.0, 0.0).astype(BF16)
        out_ref[...] = dot(onehot, x_ref[...]).astype(BF16)


def prep_kernel(
    count_ref, dst_ref, src_ref, tiles_ref, x_ref, ws_ref, wn_ref,
    rem_ref, at_ref, part_ref, self_ref, xt_ref, wst_ref, wnt_ref, a_ref,
):
    a_ref[...] = jnp.zeros_like(a_ref)
    at_ref[...] = jnp.zeros_like(at_ref)

    def place(t, carry):
        tile = tiles_ref[0, t]
        row = pl.multiple_of(dst_ref[0, t] * TILE, TILE)
        col = pl.multiple_of(src_ref[0, t] * TILE, TILE)
        a_ref[pl.ds(row, TILE), pl.ds(col, TILE)] = tile
        at_ref[pl.ds(col, TILE), pl.ds(row, TILE)] = tile.T
        return carry

    lax.fori_loop(0, count_ref[0], place, 0)
    rem_ref[...] = a_ref[:, ROWS:]
    wst_ref[...] = ws_ref[...].T
    wnt_ref[...] = wn_ref[...].T
    for i in range(ROWS // CHUNK):
        rows = slice(i * CHUNK, (i + 1) * CHUNK)
        part_ref[rows, :] = dot(a_ref[rows, :ROWS], x_ref[...])
        self_ref[rows, :] = dot(x_ref[rows, :], ws_ref[...])
        xt_ref[:, rows] = x_ref[rows, :].T


def middle_kernel(
    rem_ref, atrem_ref, bnd_ref, hub_ref, part_ref, self_ref, cot_ref, xt_ref, wn_ref, wnt_ref,
    act_ref, pg_ref, ag_ref, bg_ref, load_ref,
):
    scale = 1.0 / math.sqrt(1048576)
    gself = jnp.zeros((D, D), F32)
    gnbr = jnp.zeros((D, D), F32)
    for i in range(ROWS // CHUNK):
        rows = slice(i * CHUNK, (i + 1) * CHUNK)
        agg = (
            part_ref[rows, :]
            + dot(rem_ref[rows, :HALO], bnd_ref[...])
            + dot(rem_ref[rows, HALO:], hub_ref[...])
        ).astype(BF16)
        pre = self_ref[rows, :] + dot(agg, wn_ref[...])
        sig = jax.nn.sigmoid(pre)
        act_ref[rows, :] = (pre * sig).astype(BF16)
        pg = (cot_ref[rows, :].astype(F32) * sig * (1.0 + pre * (1.0 - sig))).astype(BF16)
        pg_ref[rows, :] = pg
        ag_ref[rows, :] = dot(pg, wnt_ref[...]).astype(BF16)
        gself = gself + dot(xt_ref[:, rows], pg)
        gnbr = gnbr + lax.dot_general(agg, pg, (((0,), (0,)), ((), ())), preferred_element_type=F32)
    bg_ref[...] = dot(atrem_ref[:HALO, :], ag_ref[...]).astype(BF16)
    hub_grad = dot(atrem_ref[HALO:, :], ag_ref[...])
    for k in range(8):
        at = k * LOAD
        grad = (gself, gnbr)[k // 4][(k % 4) * PART : (k % 4 + 1) * PART, :]
        load_ref[at : at + PART, :] = grad * scale
        load_ref[at + PART : at + LOAD, :] = hub_grad[k * HUB_DEV : (k + 1) * HUB_DEV, :]


def split_kernel(in_ref, grad_ref, hub_ref):
    total = in_ref[:LOAD, :]
    for k in range(1, 8):
        total = total + in_ref[k * LOAD : (k + 1) * LOAD, :]
    grad_ref[...] = total[:PART, :]
    hub_ref[...] = total[PART:, :]


def sum_kernel(parts, copies):
    def kernel(in_ref, *refs):
        out_ref = refs[-1]
        height = in_ref.shape[0] // parts
        total = in_ref[:height, :]
        for p in range(1, parts):
            total = total + in_ref[p * height : (p + 1) * height, :]
        total = total.astype(out_ref.dtype)
        for q in range(copies):
            out_ref[q * height : (q + 1) * height, :] = total

    return kernel


def final_kernel(send_ref, hub_ref, ret_ref, hsum_ref, pg_ref, ag_ref, wst_ref, at_ref, out_ref):
    ret = ret_ref[...]
    high = hsum_ref[...].astype(BF16)
    low = (hsum_ref[...] - high.astype(F32)).astype(BF16)
    for i in range(ROWS // CHUNK):
        rows = slice(i * CHUNK, (i + 1) * CHUNK)
        total = dot(pg_ref[rows, :], wst_ref[...]) + dot(at_ref[rows, :], ag_ref[...])
        own = lax.broadcasted_iota(jnp.int32, (CHUNK, HALO), 0) + i * CHUNK
        total = total + dot(jnp.where(own == send_ref[...], 1.0, 0.0).astype(BF16), ret)
        own = lax.broadcasted_iota(jnp.int32, (CHUNK, HUB_DEV), 0) + i * CHUNK
        hub_hot = jnp.where(own == hub_ref[...], 1.0, 0.0).astype(BF16)
        total = total + dot(hub_hot, high) + dot(hub_hot, low)
        out_ref[rows, :] = total.astype(BF16)


def per_device(
    features, cotangent, w_self, w_nbr, tile_vals, tile_dst, tile_src, tile_count, send_rows, hub_rows
):
    mib = 1 << 20
    dom = ("zh", "zl", "y")
    grp = ("x", "c")
    sent, hubs = call(
        pick_kernel, [((HALO, D), BF16), ((HUB_DEV, D), BF16)], [VM] * 3, flops=1 << 28, nbytes=mib
    )(send_rows, hub_rows, features)
    boundary = lax.all_to_all(sent, dom, 0, 0, tiled=True)
    hub_copies = lax.all_gather(hubs, grp, axis=0, tiled=True)
    rem, at, part, self_pre, xt, wst, wnt = call(
        prep_kernel,
        [
            ((ROWS, HALO + HUBS), BF16),
            ((SOURCE * TILE, ROWS), BF16),
            ((ROWS, D), F32),
            ((ROWS, D), F32),
            ((D, ROWS), BF16),
            ((D, D), BF16),
            ((D, D), BF16),
        ],
        [SM, SM, SM, VM, VM, VM, VM],
        scratch=[pltpu.VMEM((ROWS, SOURCE * TILE), BF16)],
        flops=1 << 30,
        nbytes=9 * mib,
    )(tile_count, tile_dst, tile_src, tile_vals, features, w_self, w_nbr)
    at_rem = at[ROWS:]
    act, pg, ag, bg, load = call(
        middle_kernel,
        [
            ((ROWS, D), BF16),
            ((ROWS, D), BF16),
            ((ROWS, D), BF16),
            ((HALO, D), BF16),
            ((8 * LOAD, D), F32),
        ],
        [VM] * 10,
        flops=1 << 30,
        nbytes=8 * mib,
        trans=1 << 19,
    )(rem, at_rem, boundary, hub_copies, part, self_pre, cotangent, xt, w_nbr, wnt)

    height = 2 * D // 32
    load = lax.all_to_all(load, grp, 0, 0, tiled=True)
    part, hub_sums = call(
        split_kernel, [((PART, D), F32), ((HUB_DEV, D), F32)], [VM], nbytes=mib, limit=SMALL_LIMIT
    )(load)
    part = lax.all_to_all(part, "y", 0, 0, tiled=True)
    (chunk,) = call(sum_kernel(4, 1), [((height, D), F32)], [VM], limit=SMALL_LIMIT)(part)
    bg, chunk = lax.optimization_barrier((bg.reshape(HALO // 2, 2, D), chunk))
    returned = lax.all_to_all(bg, dom, 0, 0, tiled=True).reshape(HALO, D)
    for bit in (1, 2, 4):
        chunk = chunk + lax.ppermute(chunk, "zl", [(i, i ^ bit) for i in range(ZL)])
    (chunk,) = call(sum_kernel(1, ZH), [((height * ZH, D), F32)], [VM, ANY], limit=SMALL_LIMIT)(
        chunk, returned
    )
    chunk = lax.all_to_all(chunk, "zh", 0, 0, tiled=True)
    (chunk,) = call(sum_kernel(ZH, 32), [((2 * D, D), BF16)], [VM], limit=SMALL_LIMIT)(chunk)
    grads = lax.all_to_all(chunk, ("x", "c", "y"), 0, 0, tiled=True)
    (grad_features,) = call(
        final_kernel, [((ROWS, D), BF16)], [VM] * 8, flops=1 << 30, nbytes=6 * mib
    )(send_rows, hub_rows, returned, hub_sums, pg, ag, wst, at)
    grads = grads.astype(F32)
    return act, grad_features, grads[:D], grads[D:]


def solution(mesh):
    fine = Mesh(mesh.devices.reshape(ZH, ZL, 4, 4, 2), AXES)
    whole = P(AXES, None)
    return jax.shard_map(
        per_device,
        mesh=fine,
        in_specs=(
            whole,
            whole,
            P(),
            P(),
            P(AXES, None, None, None),
            whole,
            whole,
            P(AXES),
            whole,
            whole,
        ),
        out_specs=(whole, whole, P(), P()),
        check_vma=False,
    )
```

time: 1040 us -> 206 us (0.20)
  waiting for transfers between devices: 891 us -> 14 us
  blocking collectives: 14 us -> 76.7 us
  starting transfers between devices: 54.6 us -> 85.2 us
  matrix products: 29.9 us -> 0 us
  local copies, waits for them, and re-layouts: 29.4 us -> 7.53 us
  Pallas kernels: 0 us -> 20.7 us
  between operations: 16.3 us -> 1.37 us
    psum x1 -> x0, waiting for transfers between devices: 886 us -> none  [per_device(): grad_w_self, grad_w_nbr = lax.psum((self_term, nbr_term), ('dom', 'grp'))]
    all_to_all x0 -> x2, blocking collectives: none -> 62.1 us  [the longest x1 41.6 us: per_device(): chunk = lax.all_to_all(chunk, 'zh', 0, 0, tiled=True)]
    dot_general x10 -> x0, matrix products: 29.9 us -> none  [the longest x1 5.32 us: per_device(): jnp.einsum('tb,tid->bid', dst_onehot, products, precision=lax.Precision.H...]
    pallas_call x0 -> x8, Pallas kernels: none -> 20.7 us  [the longest x1 7.31 us: per_device(): call(prep_kernel, [((ROWS, HALO + HUBS), BF16), ((SOURCE * TILE, ROWS), B...]
    ppermute x0 -> x3, starting transfers between devices: none -> 18.2 us  [per_device(): chunk = chunk + lax.ppermute(chunk, 'zl', [(i, i ^ bit) for i in range(ZL)])]
    dot_general x3 -> x0, local copies, waits for them, and re-layouts: 13.2 us -> none  [the longest x1 6.2 us: per_device(): jnp.einsum('tij,tjd->tid', tile_block, gathered, preferred_element_type=j...]
    all_to_all x2 -> x4, starting transfers between devices: 54.5 us -> 66.9 us  [the longest x1 33.9 us: per_device(): boundary = lax.all_to_all(sent, dom, 0, 0, tiled=True)]
  transfers between devices with their start and end apart: 4 -> 7, of which waited for: 2 -> 7; matrix products, arithmetic and copies ran while one was open for 2% -> 2% of each run, Pallas kernels for 0% -> 6%
where the time goes in v1:
time: 206 us
  starting transfers between devices  85.2 us (41%)
  blocking collectives  76.7 us (37%)
  Pallas kernels  20.7 us (10%)
  waiting for transfers between devices  14 us (7%)
  local copies, waits for them, and re-layouts  7.53 us (4%)
    all_to_all x1, blocking collectives, per_device(): chunk = lax.all_to_all(chunk, 'zh', 0, 0, tiled=True)  41.6 us
    all_to_all x1, starting transfers between devices, per_device(): boundary = lax.all_to_all(sent, dom, 0, 0, tiled=True)  33.9 us
    all_to_all x1, blocking collectives, per_device(): load = lax.all_to_all(load, grp, 0, 0, tiled=True)  20.5 us
    ppermute x3, starting transfers between devices, per_device(): chunk = chunk + lax.ppermute(chunk, 'zl', [(i, i ^ bit) for i in range(ZL)])  18.2 us
    all_to_all x1, starting transfers between devices, per_device(): returned = lax.all_to_all(bg, dom, 0, 0, tiled=True).reshape(HALO, D)  17.1 us
    all_gather x1, blocking collectives, per_device(): hub_copies = lax.all_gather(hubs, grp, axis=0, tiled=True)  14.7 us
    all_to_all x1, starting transfers between devices, per_device(): grads = lax.all_to_all(chunk, ('x', 'c', 'y'), 0, 0, tiled=True)  11.5 us
    pallas_call x1, Pallas kernels, per_device(): call(prep_kernel, [((ROWS, HALO + HUBS), BF16), ((SOURCE * TILE, ROWS), B...  7.31 us
  transfers between devices with their start and end apart: 7, of which 7 were waited for; matrix products, arithmetic and copies ran while one was open for 2% of the time, Pallas kernels for 6%

profile of v1, /device:TPU:1, one launch (start us, length us, event | category | flops | bytes accessed | tf_op | source)
XLA Modules:
  0.0 205.6 jit_solution(14403110402748731592)
XLA Ops:
  0.6 2.2 %shard_map.130 = (bf16[256,256]{1,0:T(8,128)(2,1)}, bf16[16,256]{1,0:T(8,128)(2,1)}) custom-call(s32[1,256]{1,0:T(1,128)} %send_ref.3, s32[1,16]{1,0:T(1,128)} %hub_ref.3, bf16[1024,256]{1,0:T(8,128)(2,1)} %x_ref.3), custom_call_target="tpu_custom_call" | custom-call | flops 268435456 | bytes 1048576 | tf_op jit(solution)/shard_map/pallas_call | solution.py:168
  2.8 1.6 all_to_all.37
  4.4 0.0 copy-start.2
  4.4 33.9 %all-to-all-start = ((bf16[128,2,256]{2,1,0:T(2,128)(2,1)}), bf16[128,2,256]{2,1,0:T(2,128)(2,1)S(1)}, u32[]{:S(2)}, u32[]{:S(2)}) async-start(bf16[128,2,256]{2,1,0:T(2,128)(2,1)} %all_to_all.37), calls=%async_computation | async-start | bytes 262144 | tf_op jit(solution)/shard_map/all_to_all | solution.py:171
  39.0 7.3 %shard_map.129 = (bf16[1024,384]{1,0:T(8,128)(2,1)}, bf16[1408,1024]{1,0:T(8,128)(2,1)}, f32[1024,256]{1,0:T(8,128)}, f32[1024,256]{1,0:T(8,128)}, bf16[256,1024...) custom-call(s32[1]{0:T(128)S(6)} %copy.14.count_ref, s32[1,40]{1,0:T(1,128)} %dst_ref.1, ...), custom_call_target="tpu_custom_call" | custom-call | flops 1073741824 | bytes 9437184 | tf_op jit(solution)/shard_map/pallas_call | solution.py:173
  46.3 2.1 %slice.15.atrem_ref = bf16[384,1024]{1,0:T(8,128)(2,1)} slice(bf16[1408,1024]{1,0:T(8,128)(2,1)} %get-tuple-element.23.at_ref), slice={[1024:1408], [0:1024]} | slice | bytes 1572864 | tf_op jit(solution)/shard_map/slice | solution.py:189
  48.4 0.0 copy-done.2
  48.4 14.7 %all_gather.3.hub_ref = bf16[128,256]{1,0:T(8,128)(2,1)} all-gather(bf16[16,256]{1,0:T(8,128)(2,1)S(1)} %copy-done.2), channel_id=1, replica_groups=mesh['zh'=4,'zl'=8,'y'=4,'x'=4,'c'=2] {'x','c'}, dimensions={0}, use_global_device_ids=true | all-gather | bytes 73728 | tf_op jit(solution)/shard_map/all_gather | solution.py:172
  63.1 0.7 all-to-all-done
  63.8 0.7 all_to_all.39.bnd_ref
  64.5 5.5 %shard_map.131 = (bf16[1024,256]{1,0:T(8,128)(2,1)}, bf16[1024,256]{1,0:T(8,128)(2,1)}, bf16[1024,256]{1,0:T(8,128)(2,1)}, bf16[256,256]{1,0:T(8,128)(2,1)}, f32[640,256]{1,0:T(8,128)}) custom-call(bf16[1024,384]{1,0:T(8,128)(2,1)} %get-tuple-element.22.rem_ref, bf16[384,1024]{1,0:T(8,128)(2,1)} %slice.15.atrem_ref, bf16[256,256]{1,0:T(8,128)(2,1)} %all_to_all.39.bnd_ref, ...), custom_call_target="tpu_custom_call" | custom-call | flops 1073741824 | bytes 8388608 | tf_op jit(solution)/shard_map/pallas_call | solution.py:190
  70.0 20.5 %all_to_all.58 = f32[8,80,256]{2,1,0:T(8,128)S(1)} all-to-all(f32[8,80,256]{2,1,0:T(8,128)} %bitcast.13), channel_id=1, replica_groups=mesh['zh'=4,'zl'=8,'y'=4,'x'=4,'c'=2] {'x','c'}, dimensions={0} | all-to-all | bytes 1310720 | tf_op jit(solution)/shard_map/all_to_all | solution.py:206
  90.5 0.7 shard_map.132
  91.1 0.0 copy-start.1
  91.1 0.6 copy-done.1
  91.7 4.4 %all-to-all-start.2 = ((f32[4,16,256]{2,1,0:T(8,128)}), f32[4,16,256]{2,1,0:T(8,128)S(1)}, u32[]{:S(2)}, u32[]{:S(2)}) async-start(f32[4,16,256]{2,1,0:T(8,128)} %bitcast.2), calls=%async_computation.2 | async-start | bytes 131072 | tf_op jit(solution)/shard_map/all_to_all | solution.py:210
  96.2 1.6 reshape.27
  97.8 2.9 %all-to-all-done.2 = f32[4,16,256]{2,1,0:T(8,128)S(1)} async-done(((f32[4,16,256]{2,1,0:T(8,128)}), f32[4,16,256]{2,1,0:T(8,128)S(1)}, u32[]{:S(2)}, u32[]{:S(2)}) %all-to-all-start.2) | async-done | bytes 65568 | tf_op jit(solution)/shard_map/all_to_all | solution.py:210
  100.6 17.1 %all-to-all-start.3 = ((bf16[128,2,256]{2,1,0:T(2,128)(2,1)}), bf16[128,2,256]{2,1,0:T(2,128)(2,1)S(1)}, u32[]{:S(2)}, u32[]{:S(2)}) async-start(bf16[128,2,256]{2,1,0:T(2,128)(2,1)} %reshape.27), calls=%async_computation.3 | async-start | bytes 262144 | tf_op jit(solution)/shard_map/all_to_all | solution.py:213
  117.8 2.5 %collective-permute-start = (f32[16,256]{1,0:T(8,128)S(1)}, f32[16,256]{1,0:T(8,128)S(1)}, u32[]{:S(2)}, u32[]{:S(2)}) collective-permute-start(f32[16,256]{1,0:T(8,128)S(1)} %shard_map.133), channel_id=1, source_target_pairs={{0,32},{32,0},{64,96},{96,64},{128,160},{160,128},{192,224},{224,1... | collective-permute-start | bytes 49160 | tf_op jit(solution)/shard_map/ppermute | solution.py:215
  120.3 2.5 %collective-permute-done = f32[16,256]{1,0:T(8,128)S(1)} collective-permute-done((f32[16,256]{1,0:T(8,128)S(1)}, f32[16,256]{1,0:T(8,128)S(1)}, u32[]{:S(2)}, u32[]{:S(2)}) %collective-permute-start) | collective-permute-done | bytes 16416 | tf_op jit(solution)/shard_map/ppermute | solution.py:215
  122.7 5.8 %collective-permute-start.1 = (f32[16,256]{1,0:T(8,128)S(1)}, f32[16,256]{1,0:T(8,128)S(1)}, u32[]{:S(2)}, u32[]{:S(2)}) collective-permute-start(f32[16,256]{1,0:T(8,128)S(1)} %add.9), channel_id=1, source_target_pairs={{0,64},{32,96},{64,0},{96,32},{128,192},{160,224},{192,128},{224,1... | collective-permute-start | bytes 49160 | tf_op jit(solution)/shard_map/ppermute | solution.py:215
  128.5 1.7 collective-permute-done.1
  130.2 10.0 %collective-permute-start.2 = (f32[16,256]{1,0:T(8,128)S(1)}, f32[16,256]{1,0:T(8,128)S(1)}, u32[]{:S(2)}, u32[]{:S(2)}) collective-permute-start(f32[16,256]{1,0:T(8,128)S(1)} %add.10), channel_id=1, source_target_pairs={{0,128},{32,160},{64,192},{96,224},{128,0},{160,32},{192,64},{224,... | collective-permute-start | bytes 49160 | tf_op jit(solution)/shard_map/ppermute | solution.py:215
  140.2 1.4 collective-permute-done.2
  141.6 0.4 all-to-all-done.3
  142.1 0.1 reshape.28.ret_ref.refs_0_
  142.1 0.0 copy-start
  142.2 41.6 %all_to_all.59 = f32[4,16,256]{2,1,0:T(8,128)S(1)} all-to-all(f32[4,16,256]{2,1,0:T(8,128)S(1)} %bitcast.12), channel_id=1, replica_groups=mesh['zh'=4,'zl'=8,'y'=4,'x'=4,'c'=2] {'zh'}, dimensions={0} | all-to-all | bytes 131072 | tf_op jit(solution)/shard_map/all_to_all | solution.py:219
  183.7 0.7 shard_map.136
  184.5 11.5 %all-to-all-start.5 = ((bf16[32,16,256]{2,1,0:T(8,128)(2,1)}), bf16[32,16,256]{2,1,0:T(8,128)(2,1)S(1)}, u32[]{:S(2)}, u32[]{:S(2)}) async-start(bf16[32,16,256]{2,1,0:T(8,128)(2,1)} %bitcast.6), calls=%async_computation.5 | async-start | bytes 524288 | tf_op jit(solution)/shard_map/all_to_all | solution.py:221
  195.9 0.0 copy-done
  195.9 4.3 %shard_map.134 = bf16[1024,256]{1,0:T(8,128)(2,1)} custom-call(s32[1,256]{1,0:T(1,128)} %send_ref.3, s32[1,16]{1,0:T(1,128)} %hub_ref.3, bf16[256,256]{1,0:T(8,128)(2,1)} %copy-done, f32[16,256]{1,0:T(8,128)} %copy-done.1, bf16[1024,256]{1,0:T(8,128)(2,1)} %get-tuple-element.36.pg_ref, bf16[1024,256]{1,0:T(8,128)(2,1)} %get-tuple-element.37.ag_ref, ...), custom_call_target="tpu_custom_call" | custom-call | flops 1073741824 | bytes 6291456 | tf_op jit(solution)/shard_map/pallas_call | solution.py:222
  200.3 4.5 %all-to-all-done.5 = bf16[32,16,256]{2,1,0:T(8,128)(2,1)S(1)} async-done(((bf16[32,16,256]{2,1,0:T(8,128)(2,1)}), bf16[32,16,256]{2,1,0:T(8,128)(2,1)S(1)}, u32[]{:S(2)}, u32[]{:S(2)}) %all-to-all-start.5) | async-done | bytes 262176 | tf_op jit(solution)/shard_map/all_to_all | solution.py:221
  204.7 0.8 fusion
  (5 shorter events, 0.0 us)
Async XLA Ops:
  4.4 43.9 %copy-start.2 = (bf16[16,256]{1,0:T(8,128)(2,1)S(1)}, bf16[16,256]{1,0:T(8,128)(2,1)}, u32[]{:S(2)}) copy-start(bf16[16,256]{1,0:T(8,128)(2,1)} %get-tuple-element.25) | copy-start | bytes 24580
  4.4 59.3 %all-to-all-start = ((bf16[128,2,256]{2,1,0:T(2,128)(2,1)}), bf16[128,2,256]{2,1,0:T(2,128)(2,1)S(1)}, u32[]{:S(2)}, u32[]{:S(2)}) async-start(bf16[128,2,256]{2,1,0:T(2,128)(2,1)} %all_to_all.37), calls=%async_computation | async-start | bytes 262144 | tf_op jit(solution)/shard_map/all_to_all | solution.py:171
  91.1 0.6 copy-start.1
  91.7 8.9 %all-to-all-start.2 = ((f32[4,16,256]{2,1,0:T(8,128)}), f32[4,16,256]{2,1,0:T(8,128)S(1)}, u32[]{:S(2)}, u32[]{:S(2)}) async-start(f32[4,16,256]{2,1,0:T(8,128)} %bitcast.2), calls=%async_computation.2 | async-start | bytes 131072 | tf_op jit(solution)/shard_map/all_to_all | solution.py:210
  100.6 41.4 %all-to-all-start.3 = ((bf16[128,2,256]{2,1,0:T(2,128)(2,1)}), bf16[128,2,256]{2,1,0:T(2,128)(2,1)S(1)}, u32[]{:S(2)}, u32[]{:S(2)}) async-start(bf16[128,2,256]{2,1,0:T(2,128)(2,1)} %reshape.27), calls=%async_computation.3 | async-start | bytes 262144 | tf_op jit(solution)/shard_map/all_to_all | solution.py:213
  117.8 4.9 %collective-permute-start = (f32[16,256]{1,0:T(8,128)S(1)}, f32[16,256]{1,0:T(8,128)S(1)}, u32[]{:S(2)}, u32[]{:S(2)}) collective-permute-start(f32[16,256]{1,0:T(8,128)S(1)} %shard_map.133), channel_id=1, source_target_pairs={{0,32},{32,0},{64,96},{96,64},{128,160},{160,128},{192,224},{224,1... | collective-permute-start | bytes 49160 | tf_op jit(solution)/shard_map/ppermute | solution.py:215
  122.7 7.5 %collective-permute-start.1 = (f32[16,256]{1,0:T(8,128)S(1)}, f32[16,256]{1,0:T(8,128)S(1)}, u32[]{:S(2)}, u32[]{:S(2)}) collective-permute-start(f32[16,256]{1,0:T(8,128)S(1)} %add.9), channel_id=1, source_target_pairs={{0,64},{32,96},{64,0},{96,32},{128,192},{160,224},{192,128},{224,1... | collective-permute-start | bytes 49160 | tf_op jit(solution)/shard_map/ppermute | solution.py:215
  130.2 11.4 %collective-permute-start.2 = (f32[16,256]{1,0:T(8,128)S(1)}, f32[16,256]{1,0:T(8,128)S(1)}, u32[]{:S(2)}, u32[]{:S(2)}) collective-permute-start(f32[16,256]{1,0:T(8,128)S(1)} %add.10), channel_id=1, source_target_pairs={{0,128},{32,160},{64,192},{96,224},{128,0},{160,32},{192,64},{224,... | collective-permute-start | bytes 49160 | tf_op jit(solution)/shard_map/ppermute | solution.py:215
  142.1 53.8 %copy-start = (bf16[256,256]{1,0:T(8,128)(2,1)}, bf16[256,256]{1,0:T(8,128)(2,1)S(1)}, u32[]{:S(2)}) copy-start(bf16[256,256]{1,0:T(8,128)(2,1)S(1)} %reshape.28.ret_ref.refs_0_) | copy-start | bytes 393220
  184.5 20.3 %all-to-all-start.5 = ((bf16[32,16,256]{2,1,0:T(8,128)(2,1)}), bf16[32,16,256]{2,1,0:T(8,128)(2,1)S(1)}, u32[]{:S(2)}, u32[]{:S(2)}) async-start(bf16[32,16,256]{2,1,0:T(8,128)(2,1)} %bitcast.6), calls=%async_computation.5 | async-start | bytes 524288 | tf_op jit(solution)/shard_map/all_to_all | solution.py:221

commit v2 on v1

v2 whole, which is shorter than its diff:
```python
import math

import jax
import jax.numpy as jnp
import numpy as np
from jax import lax
from jax.experimental import pallas as pl
from jax.experimental.pallas import tpu as pltpu
from jax.sharding import Mesh
from jax.sharding import PartitionSpec as P

TILE = 128
ROWS = 1024
HALO = 256
HUBS = 128
HUB_DEV = 16
PART = 128
HALF = 128
LOAD = PART + 2 * HUB_DEV
LOCAL = 8
SOURCE = 11
TILES = 40
D = 256
PACK = D + HALF
TURN = HALO // 2
CHUNK = 256
ZL = 4
ZH = 8
NEAR = 16
FAR = 40
ALONG = np.arange(1024).reshape(ZH, ZL, 4, 4, 2)


def groups(order, turn=0):
    others = [axis for axis in range(5) if axis not in order]
    table = ALONG.transpose(others + list(order))
    table = np.roll(table, -turn, axis=len(others))
    return table.reshape(-1, math.prod(ALONG.shape[axis] for axis in order)).tolist()


def swap_rows(array, order, turn=0):
    return lax.all_to_all(array, "d", 0, 0, axis_index_groups=groups(order, turn), tiled=True)


BF16 = jnp.bfloat16
F32 = jnp.float32
VMEM_LIMIT = 60 * 1024 * 1024
SMALL_LIMIT = 16 * 1024 * 1024

VM = pl.BlockSpec(memory_space=pltpu.VMEM)
SM = pl.BlockSpec(memory_space=pltpu.SMEM)


def dot(a, b):
    return jnp.dot(a, b, preferred_element_type=F32)


def call(kernel, outs, specs, scratch=(), flops=0, nbytes=0, trans=0, limit=VMEM_LIMIT):
    return pl.pallas_call(
        kernel,
        out_shape=[jax.ShapeDtypeStruct(s, t) for s, t in outs],
        in_specs=list(specs),
        out_specs=[VM] * len(outs),
        scratch_shapes=list(scratch),
        compiler_params=pltpu.CompilerParams(vmem_limit_bytes=limit),
        cost_estimate=pl.CostEstimate(flops=flops, bytes_accessed=nbytes, transcendentals=trans),
    )


def column_of(row, count):
    here = lax.broadcasted_iota(jnp.int32, (count, count), 0)
    there = lax.broadcasted_iota(jnp.int32, (count, count), 1)
    spread = jnp.where(here == there, jnp.broadcast_to(row, (count, count)).astype(F32), 0.0)
    return jnp.sum(spread, axis=1, keepdims=True).astype(jnp.int32)


def permute(first, second, turn=0):
    to = lax.broadcasted_iota(jnp.int32, (HALO, HALO), 0)
    at = lax.broadcasted_iota(jnp.int32, (HALO, HALO), 1)
    inner, pair = to // 2 % first, (to // (2 * first) + turn) % second
    return jnp.where(at == (inner * second + pair) * 2 + to % 2, 1.0, 0.0).astype(BF16)


def halves(value):
    high = value.astype(BF16).astype(F32)
    return jnp.concatenate([high, value - high], axis=0).astype(BF16)


def pick_kernel(send_ref, hub_ref, x_ref, sent_ref, hubs_ref):
    def picked(idx_ref):
        count = idx_ref.shape[1]
        column = column_of(idx_ref[...], count)
        lanes = lax.broadcasted_iota(jnp.int32, (count, ROWS), 1)
        onehot = jnp.where(lanes == column, 1.0, 0.0).astype(BF16)
        return dot(onehot, x_ref[...]).astype(BF16)

    sent = picked(send_ref)
    sent_ref[:TURN, :] = sent[TURN:, :]
    sent_ref[TURN:, :] = sent[:TURN, :]
    hubs_ref[...] = picked(hub_ref)


def prep_kernel(
    count_ref, dst_ref, src_ref, tiles_ref, x_ref, ws_ref, wn_ref,
    rem_ref, atrem_ref, part_ref, self_ref, xt_ref, wnt_ref, a_ref, far_ref,
):
    a_ref[...] = jnp.zeros_like(a_ref)
    far_ref[...] = jnp.zeros_like(far_ref)

    def place(t, carry):
        row = pl.multiple_of(dst_ref[0, t] * TILE, TILE)
        source = src_ref[0, t]
        a_ref[pl.ds(row, TILE), pl.ds(pl.multiple_of(source * TILE, TILE), TILE)] = tiles_ref[0, t]

        @pl.when(source >= LOCAL)
        def _():
            col = pl.multiple_of((source - LOCAL) * TILE, TILE)
            far_ref[pl.ds(col, TILE), pl.ds(row, TILE)] = tiles_ref[0, t].T

        return carry

    lax.fori_loop(0, count_ref[0], place, 0)
    rem_ref[:, :TURN] = a_ref[:, ROWS + TURN : ROWS + HALO]
    rem_ref[:, TURN:HALO] = a_ref[:, ROWS : ROWS + TURN]
    rem_ref[:, HALO:] = a_ref[:, ROWS + HALO :]
    atrem_ref[:HALO, :] = dot(permute(ZH, NEAR), far_ref[:HALO, :]).astype(BF16)
    atrem_ref[HALO:, :] = far_ref[HALO:, :]
    wnt_ref[...] = wn_ref[...].T
    for i in range(ROWS // CHUNK):
        rows = slice(i * CHUNK, (i + 1) * CHUNK)
        part_ref[rows, :] = dot(a_ref[rows, :ROWS], x_ref[...])
        self_ref[rows, :] = dot(x_ref[rows, :], ws_ref[...])
        xt_ref[:, rows] = x_ref[rows, :].T


def middle_kernel(
    rem_ref, atrem_ref, bnd_ref, hub_ref, part_ref, self_ref, cot_ref, xt_ref, wn_ref, wnt_ref,
    act_ref, pg_ref, ag_ref, bg_ref, load_ref,
):
    scale = 1.0 / math.sqrt(1048576)
    gself = jnp.zeros((D, D), F32)
    gnbr = jnp.zeros((D, D), F32)
    for i in range(ROWS // CHUNK):
        rows = slice(i * CHUNK, (i + 1) * CHUNK)
        agg = (
            part_ref[rows, :]
            + dot(rem_ref[rows, :HALO], bnd_ref[...])
            + dot(rem_ref[rows, HALO:], hub_ref[...])
        ).astype(BF16)
        pre = self_ref[rows, :] + dot(agg, wn_ref[...])
        sig = jax.nn.sigmoid(pre)
        act_ref[rows, :] = (pre * sig).astype(BF16)
        pg = (cot_ref[rows, :].astype(F32) * sig * (1.0 + pre * (1.0 - sig))).astype(BF16)
        pg_ref[rows, :] = pg
        ag_ref[rows, :] = dot(pg, wnt_ref[...]).astype(BF16)
        gself = gself + dot(xt_ref[:, rows], pg)
        gnbr = gnbr + lax.dot_general(agg, pg, (((0,), (0,)), ((), ())), preferred_element_type=F32)
    bg_ref[...] = dot(atrem_ref[:HALO, :], ag_ref[...]).astype(BF16)
    hub_grad = dot(atrem_ref[HALO:, :], ag_ref[...])
    for k in range(8):
        lanes = slice(k // 4 * HALF, (k // 4 + 1) * HALF)
        rows = slice(k % 2 * PART, (k % 2 + 1) * PART)
        at = k * LOAD
        load_ref[at : at + PART, :] = (gself, gnbr)[k // 2 % 2][rows, lanes] * scale
        hub = hub_grad[k * HUB_DEV : (k + 1) * HUB_DEV, :]
        load_ref[at + PART : at + PART + HUB_DEV, :] = hub[:, :HALF]
        load_ref[at + PART + HUB_DEV : at + LOAD, :] = hub[:, HALF:]


def near_kernel(in_ref, bg_ref, out_ref, hub_ref):
    total = in_ref[:LOAD, :]
    for k in range(1, 8):
        total = total + in_ref[k * LOAD : (k + 1) * LOAD, :]
    hub_ref[:, :HALF] = total[PART : PART + HUB_DEV, :]
    hub_ref[:, HALF:] = total[PART + HUB_DEV :, :]
    out_ref[:, :D] = bg_ref[...]
    for m in range(NEAR):
        out_ref[m * 16 : (m + 1) * 16, D:] = halves(total[m * 8 : (m + 1) * 8, :])


def far_kernel(in_ref, out_ref):
    total = in_ref[:16, D:].astype(F32)
    for m in range(1, NEAR):
        total = total + in_ref[m * 16 : (m + 1) * 16, D:].astype(F32)
    chunk = total[:8, :] + total[8:, :]
    high = chunk.astype(BF16).astype(F32)
    both = jnp.concatenate([high, chunk - high], axis=1)
    moved = dot(permute(NEAR, ZH, ZH // 2), in_ref[:, :D])
    for j in range(ZH // 2):
        block = [moved[j * 64 : j * 64 + 32, :], both, moved[j * 64 + 32 : j * 64 + 64, :], both]
        out_ref[j * 2 * FAR : (j + 1) * 2 * FAR, :] = jnp.concatenate(block, axis=0).astype(BF16)


def far_blocks(in_ref):
    for j in range(ZH // 2):
        block = in_ref[j * 2 * FAR : (j + 1) * 2 * FAR, :].astype(F32)
        yield block[:FAR, :]
        yield block[FAR:, :]


def spread_kernel(in_ref, out_ref):
    total = jnp.zeros((8, D), F32)
    for block in far_blocks(in_ref):
        total = total + block[32:, :]
    chunk = total[:, :HALF] + total[:, HALF:]
    both = jnp.concatenate([chunk, chunk], axis=0).astype(BF16)
    for q in range(out_ref.shape[0] // 16):
        out_ref[q * 16 : (q + 1) * 16, :] = both


def final_kernel(
    count_ref, dst_ref, src_ref, send_ref, hub_ref, ret_ref, hsum_ref, pg_ref, ag_ref, ws_ref, tiles_ref,
    out_ref, at_ref,
):
    at_ref[...] = jnp.zeros_like(at_ref)

    def place(t, carry):
        source = src_ref[0, t]

        @pl.when(source < LOCAL)
        def _():
            row = pl.multiple_of(source * TILE, TILE)
            col = pl.multiple_of(dst_ref[0, t] * TILE, TILE)
            at_ref[pl.ds(row, TILE), pl.ds(col, TILE)] = tiles_ref[0, t].T

        return carry

    lax.fori_loop(0, count_ref[0], place, 0)
    blocks = [block[:32, :] for block in far_blocks(ret_ref)]
    ret = jnp.concatenate(blocks[ZH // 2 :] + blocks[: ZH // 2], axis=0).astype(BF16)
    high = hsum_ref[...].astype(BF16)
    low = (hsum_ref[...] - high.astype(F32)).astype(BF16)
    wst = ws_ref[...].T
    for i in range(ROWS // CHUNK):
        rows = slice(i * CHUNK, (i + 1) * CHUNK)
        total = dot(pg_ref[rows, :], wst) + dot(at_ref[rows, :], ag_ref[...])
        own = lax.broadcasted_iota(jnp.int32, (CHUNK, HALO), 0) + i * CHUNK
        total = total + dot(jnp.where(own == send_ref[...], 1.0, 0.0).astype(BF16), ret)
        own = lax.broadcasted_iota(jnp.int32, (CHUNK, HUB_DEV), 0) + i * CHUNK
        hub_hot = jnp.where(own == hub_ref[...], 1.0, 0.0).astype(BF16)
        total = total + dot(hub_hot, high) + dot(hub_hot, low)
        out_ref[rows, :] = total.astype(BF16)


def per_device(
    features, cotangent, w_self, w_nbr, tile_vals, tile_dst, tile_src, tile_count, send_rows, hub_rows
):
    mib = 1 << 20
    sent, hubs = call(
        pick_kernel, [((HALO, D), BF16), ((HUB_DEV, D), BF16)], [VM] * 3, flops=1 << 28, nbytes=mib
    )(send_rows, hub_rows, features)
    boundary = swap_rows(sent, (0, 1, 2), ZH // 2)
    hub_copies = hubs
    for axis in (4, 3):
        hub_copies = lax.all_gather(hub_copies, "d", axis_index_groups=groups((axis,)), axis=0, tiled=True)
    rem, at_rem, part, self_pre, xt, wnt = call(
        prep_kernel,
        [
            ((ROWS, HALO + HUBS), BF16),
            ((HALO + HUBS, ROWS), BF16),
            ((ROWS, D), F32),
            ((ROWS, D), F32),
            ((D, ROWS), BF16),
            ((D, D), BF16),
        ],
        [SM, SM, SM, VM, VM, VM, VM],
        scratch=[pltpu.VMEM((ROWS, SOURCE * TILE), BF16), pltpu.VMEM((HALO + HUBS, ROWS), BF16)],
        flops=1 << 30,
        nbytes=9 * mib,
    )(tile_count, tile_dst, tile_src, tile_vals, features, w_self, w_nbr)
    act, pg, ag, bg, load = call(
        middle_kernel,
        [
            ((ROWS, D), BF16),
            ((ROWS, D), BF16),
            ((ROWS, D), BF16),
            ((HALO, D), BF16),
            ((8 * LOAD, HALF), F32),
        ],
        [VM] * 10,
        flops=1 << 30,
        nbytes=8 * mib,
        trans=1 << 19,
    )(rem, at_rem, boundary, hub_copies, part, self_pre, cotangent, xt, w_nbr, wnt)

    load = swap_rows(load, (3, 4))
    near, hub_sums = call(
        near_kernel, [((HALO, PACK), BF16), ((HUB_DEV, D), F32)], [VM] * 2, nbytes=mib, limit=SMALL_LIMIT
    )(load, bg)
    near = swap_rows(near, (1, 2))
    (far,) = call(far_kernel, [((ZH * FAR, D), BF16)], [VM], nbytes=mib, limit=SMALL_LIMIT)(near)
    returned = swap_rows(far, (0,), ZH // 2)
    (chunk,) = call(spread_kernel, [((4 * D, HALF), BF16)], [VM], nbytes=mib, limit=SMALL_LIMIT)(returned)
    grads = swap_rows(chunk, (3, 4, 1, 2))
    (grad_features,) = call(
        final_kernel,
        [((ROWS, D), BF16)],
        [SM] * 3 + [VM] * 8,
        scratch=[pltpu.VMEM((ROWS, ROWS), BF16)],
        flops=1 << 30,
        nbytes=5 * mib,
    )(tile_count, tile_dst, tile_src, send_rows, hub_rows, returned, hub_sums, pg, ag, w_self, tile_vals)
    grads = grads.astype(F32).reshape(2, 2, D, HALF)
    grads = jnp.concatenate([grads[0], grads[1]], axis=2)
    return act, grad_features, grads[0], grads[1]


def solution(mesh):
    whole = P("d", None)
    return jax.shard_map(
        per_device,
        mesh=Mesh(mesh.devices.reshape(-1), ("d",)),
        in_specs=(
            whole,
            whole,
            P(),
            P(),
            P("d", None, None, None),
            whole,
            whole,
            P("d"),
            whole,
            whole,
        ),
        out_specs=(whole, whole, P(), P()),
        check_vma=False,
    )
```

time: 206 us -> 158 us (0.77)
  starting transfers between devices: 85.2 us -> 47.9 us
  waiting for transfers between devices: 14 us -> 8.15 us
  local copies, waits for them, and re-layouts: 7.53 us -> 2.37 us
  Pallas kernels: 20.7 us -> 18.6 us
    all_to_all x4 -> x2, starting transfers between devices: 66.9 us -> 47.9 us  [swap_rows(): lax.all_to_all(array, 'd', 0, 0, axis_index_groups=groups(order, turn), t...]
    ppermute x3 -> x0, starting transfers between devices: 18.2 us -> none  [per_device(): chunk = chunk + lax.ppermute(chunk, 'zl', [(i, i ^ bit) for i in range(ZL)])]
    ppermute x3 -> x0, waiting for transfers between devices: 5.56 us -> none  [per_device(): chunk = chunk + lax.ppermute(chunk, 'zl', [(i, i ^ bit) for i in range(ZL)])]
    all_to_all x2 -> x3, blocking collectives: 62.1 us -> 65.1 us  [swap_rows(): lax.all_to_all(array, 'd', 0, 0, axis_index_groups=groups(order, turn), t...]
    slice x2 -> x1, local copies, waits for them, and re-layouts: 2.93 us -> 0.04 us  [per_device(): grads = jnp.concatenate([grads[0], grads[1]], axis=2)]
    pallas_call x6 -> x5, Pallas kernels: 13 us -> 10.9 us  [the longest x1 5.24 us: per_device(): call(prep_kernel, [((ROWS, HALO + HUBS), BF16), ((HALO + HUBS, ROWS), BF1...]
    all_gather x1 -> x2, blocking collectives: 14.7 us -> 13.6 us  [per_device(): lax.all_gather(hub_copies, 'd', axis_index_groups=groups((axis,)), axis=0...]
    all_to_all x4 -> x2, waiting for transfers between devices: 8.46 us -> 8.15 us  [swap_rows(): lax.all_to_all(array, 'd', 0, 0, axis_index_groups=groups(order, turn), t...]
  transfers between devices with their start and end apart: 7 -> 2, of which waited for: 7 -> 1; matrix products, arithmetic and copies ran while one was open for 2% -> 0% of each run, Pallas kernels for 6% -> 6%
where the time goes in v2:
time: 158 us
  blocking collectives  78.7 us (50%)
  starting transfers between devices  47.9 us (30%)
  Pallas kernels  18.6 us (12%)
  waiting for transfers between devices  8.15 us (5%)
  local copies, waits for them, and re-layouts  2.37 us (2%)
    all_to_all x3, blocking collectives, swap_rows(): lax.all_to_all(array, 'd', 0, 0, axis_index_groups=groups(order, turn), t...  65.1 us
    all_to_all x2, starting transfers between devices, swap_rows(): lax.all_to_all(array, 'd', 0, 0, axis_index_groups=groups(order, turn), t...  47.9 us
    all_gather x2, blocking collectives, per_device(): lax.all_gather(hub_copies, 'd', axis_index_groups=groups((axis,)), axis=0...  13.6 us
    all_to_all x2, waiting for transfers between devices, swap_rows(): lax.all_to_all(array, 'd', 0, 0, axis_index_groups=groups(order, turn), t...  8.15 us
    pallas_call x1, Pallas kernels, per_device(): call(middle_kernel, [((ROWS, D), BF16), ((ROWS, D), BF16), ((ROWS, D), BF...  5.49 us
    pallas_call x1, Pallas kernels, per_device(): call(prep_kernel, [((ROWS, HALO + HUBS), BF16), ((HALO + HUBS, ROWS), BF1...  5.24 us
    pallas_call x1, Pallas kernels, per_device(): call(final_kernel, [((ROWS, D), BF16)], [SM] * 3 + [VM] * 8, scratch=[plt...  4.7 us
  transfers between devices with their start and end apart: 2, of which 1 were waited for; matrix products, arithmetic and copies ran while one was open for 0% of the time, Pallas kernels for 6%

profile of v2, /device:TPU:1, one launch (start us, length us, event | category | flops | bytes accessed | tf_op | source)
XLA Modules:
  0.0 157.9 jit_solution(3021073733563573297)
XLA Ops:
  0.6 2.2 %shard_map.130 = (bf16[256,256]{1,0:T(8,128)(2,1)}, bf16[16,256]{1,0:T(8,128)(2,1)}) custom-call(s32[1,256]{1,0:T(1,128)} %send_ref.3, s32[1,16]{1,0:T(1,128)} %hub_ref.3, bf16[1024,256]{1,0:T(8,128)(2,1)} %x_ref.3), custom_call_target="tpu_custom_call" | custom-call | flops 268435456 | bytes 1048576 | tf_op jit(solution)/shard_map/pallas_call | solution.py:249
  2.8 1.6 %all_to_all.34 = bf16[128,2,256]{2,1,0:T(2,128)(2,1)} reshape(bf16[256,256]{1,0:T(8,128)(2,1)} %get-tuple-element.21) | data formatting | bytes 262144 | tf_op jit(solution)/shard_map/all_to_all | solution.py:42
  4.4 40.3 %all-to-all-start = ((bf16[128,2,256]{2,1,0:T(2,128)(2,1)}), bf16[128,2,256]{2,1,0:T(2,128)(2,1)S(1)}, u32[]{:S(2)}, u32[]{:S(2)}) async-start(bf16[128,2,256]{2,1,0:T(2,128)(2,1)} %all_to_all.34), calls=%async_computation | async-start | bytes 262144 | tf_op jit(solution)/shard_map/all_to_all | solution.py:42
  45.4 2.9 %all_gather.6 = bf16[32,256]{1,0:T(8,128)(2,1)S(1)} all-gather(bf16[16,256]{1,0:T(8,128)(2,1)} %get-tuple-element.22), channel_id=1, replica_groups={{0,1},{2,3},{4,5},{6,7},{8,9},{10,11},{12,13},{14,15},{16,17},{18,19},{..., dimensions={0}, use_global_device_ids=true | all-gather | bytes 24576 | tf_op jit(solution)/shard_map/all_gather | solution.py:255
  48.3 10.6 %all_gather.7.hub_ref = bf16[128,256]{1,0:T(8,128)(2,1)} all-gather(bf16[32,256]{1,0:T(8,128)(2,1)S(1)} %all_gather.6), channel_id=1, replica_groups={{0,2,4,6},{1,3,5,7},{8,10,12,14},{9,11,13,15},{16,18,20,22},{17,19,21,2..., dimensions={0}, use_global_device_ids=true | all-gather | bytes 81920 | tf_op jit(solution)/shard_map/all_gather | solution.py:255
  58.9 5.2 %shard_map.129 = (bf16[1024,384]{1,0:T(8,128)(2,1)}, bf16[384,1024]{1,0:T(8,128)(2,1)}, f32[1024,256]{1,0:T(8,128)}, f32[1024,256]{1,0:T(8,128)}, bf16[256,1024]{1,0:T(8,128)(2,1)}, /*index=5*/bf16[256,256]{1,0:T(8,128)(2,1)}) custom-call(s32[1]{0:T(128)S(6)} %copy.14.count_ref, s32[1,40]{1,0:T(1,128)} %dst_ref.3, s32[1,40]{1,0:T(1,128)} %src_ref.3, ...), custom_call_target="tpu_custom_call" | custom-call | flops 1073741824 | bytes 9437184 | tf_op jit(solution)/shard_map/pallas_call | solution.py:256
  64.2 0.0 all-to-all-done
  64.2 0.7 all_to_all.36.bnd_ref
  64.9 5.5 %shard_map.131 = (bf16[1024,256]{1,0:T(8,128)(2,1)}, bf16[1024,256]{1,0:T(8,128)(2,1)}, bf16[1024,256]{1,0:T(8,128)(2,1)}, bf16[256,256]{1,0:T(8,128)(2,1)}, f32[1280,128]{1,0:T(8,128)}) custom-call(bf16[1024,384]{1,0:T(8,128)(2,1)} %get-tuple-element.19.rem_ref, bf16[384,1024]{1,0:T(8,128)(2,1)} %get-tuple-element.20.atrem_ref, ...), custom_call_target="tpu_custom_call" | custom-call | flops 1073741824 | bytes 8388608 | tf_op jit(solution)/shard_map/pallas_call | solution.py:271
  70.4 0.0 copy-start.1
  70.4 17.7 %all_to_all.53 = f32[8,160,128]{2,1,0:T(8,128)S(1)} all-to-all(f32[8,160,128]{2,1,0:T(8,128)} %bitcast.21), channel_id=1, replica_groups={{0,1,2,3,4,5,6,7},{8,9,10,11,12,13,14,15},{16,17,18,19,20,21,22,23},{24..., dimensions={0} | all-to-all | bytes 1310720 | tf_op jit(solution)/shard_map/all_to_all | solution.py:42
  88.1 0.0 copy-done.1
  88.1 0.0 copy-start.2
  88.1 12.6 %all_to_all.54 = bf16[16,16,384]{2,1,0:T(8,128)(2,1)S(1)} all-to-all(bf16[16,16,384]{2,1,0:T(8,128)(2,1)S(1)} %bitcast.18), channel_id=1, replica_groups={{0,8,16,24,32,40,48,56,64,72,80,88,96,104,112,120},{1,9,17,25,33,41,49,..., dimensions={0} | all-to-all | bytes 393216 | tf_op jit(solution)/shard_map/all_to_all | solution.py:42
  100.7 0.2 shard_map.133
  100.9 34.9 %all_to_all.55 = bf16[8,40,256]{2,1,0:T(8,128)(2,1)S(1)} all-to-all(bf16[8,40,256]{2,1,0:T(8,128)(2,1)S(1)} %bitcast.17), channel_id=1, replica_groups={{512,640,768,896,0,128,256,384},{513,641,769,897,1,129,257,385},{514,64..., dimensions={0} | all-to-all | bytes 327680 | tf_op jit(solution)/shard_map/all_to_all | solution.py:42
  135.8 0.0 copy-done.2
  135.8 0.0 copy-start
  135.8 0.8 shard_map.135
  136.6 7.6 %all-to-all-start.4 = ((bf16[128,8,128]{2,1,0:T(8,128)(2,1)}), bf16[128,8,128]{2,1,0:T(8,128)(2,1)S(1)}, u32[]{:S(2)}, u32[]{:S(2)}) async-start(bf16[128,8,128]{2,1,0:T(8,128)(2,1)} %bitcast.6), calls=%async_computation.4 | async-start | bytes 524288 | tf_op jit(solution)/shard_map/all_to_all | solution.py:42
  144.2 0.0 copy-done
  144.2 4.7 %shard_map.134 = bf16[1024,256]{1,0:T(8,128)(2,1)} custom-call(s32[1]{0:T(128)S(6)} %copy.14.count_ref, s32[1,40]{1,0:T(1,128)} %dst_ref.3, s32[1,40]{1,0:T(1,128)} %src_ref.3, s32[1,256]{1,0:T(1,128)} %send_ref.3, s32[1,16]{1,0:T(1,128)} %hub_ref.3, bf16[320,256]{1,0:T(8,128)(2,1)} %bitcast.16, f32[16,256]{1,0:T(8,128)} %copy-done.2, ...), custom_call_target="tpu_custom_call" | custom-call | flops 1073741824 | bytes 5242880 | tf_op jit(solution)/shard_map/pallas_call | solution.py:295
  148.9 8.1 %all-to-all-done.4 = bf16[128,8,128]{2,1,0:T(8,128)(2,1)S(1)} async-done(((bf16[128,8,128]{2,1,0:T(8,128)(2,1)}), bf16[128,8,128]{2,1,0:T(8,128)(2,1)S(1)}, u32[]{:S(2)}, u32[]{:S(2)}) %all-to-all-start.4) | async-done | bytes 262176 | tf_op jit(solution)/shard_map/all_to_all | solution.py:42
  157.1 0.8 fusion.2
  (2 shorter events, 0.1 us)
Async XLA Ops:
  4.4 59.7 %all-to-all-start = ((bf16[128,2,256]{2,1,0:T(2,128)(2,1)}), bf16[128,2,256]{2,1,0:T(2,128)(2,1)S(1)}, u32[]{:S(2)}, u32[]{:S(2)}) async-start(bf16[128,2,256]{2,1,0:T(2,128)(2,1)} %all_to_all.34), calls=%async_computation | async-start | bytes 262144 | tf_op jit(solution)/shard_map/all_to_all | solution.py:42
  70.4 17.7 %copy-start.1 = (bf16[256,256]{1,0:T(8,128)(2,1)S(1)}, bf16[256,256]{1,0:T(8,128)(2,1)}, u32[]{:S(2)}) copy-start(bf16[256,256]{1,0:T(8,128)(2,1)} %get-tuple-element.29.bg_ref) | copy-start | bytes 393220
  88.1 47.7 %copy-start.2 = (f32[16,256]{1,0:T(8,128)}, f32[16,256]{1,0:T(8,128)S(1)}, u32[]{:S(2)}) copy-start(f32[16,256]{1,0:T(8,128)S(1)} %get-tuple-element.31.hsum_ref) | copy-start | bytes 49156
  135.8 8.4 %copy-start = (bf16[8,40,256]{2,1,0:T(8,128)(2,1)}, bf16[8,40,256]{2,1,0:T(8,128)(2,1)S(1)}, u32[]{:S(2)}) copy-start(bf16[8,40,256]{2,1,0:T(8,128)(2,1)S(1)} %all_to_all.55) | copy-start | bytes 491524
  136.6 20.5 %all-to-all-start.4 = ((bf16[128,8,128]{2,1,0:T(8,128)(2,1)}), bf16[128,8,128]{2,1,0:T(8,128)(2,1)S(1)}, u32[]{:S(2)}, u32[]{:S(2)}) async-start(bf16[128,8,128]{2,1,0:T(8,128)(2,1)} %bitcast.6), calls=%async_computation.4 | async-start | bytes 524288 | tf_op jit(solution)/shard_map/all_to_all | solution.py:42

commit v3 on v2

--- a/solution.py
+++ b/solution.py
@@ -92,12 +92,12 @@
         column = column_of(idx_ref[...], count)
         lanes = lax.broadcasted_iota(jnp.int32, (count, ROWS), 1)
         onehot = jnp.where(lanes == column, 1.0, 0.0).astype(BF16)
-        return dot(onehot, x_ref[...]).astype(BF16)
+        return dot(onehot, x_ref[...])
 
     sent = picked(send_ref)
-    sent_ref[:TURN, :] = sent[TURN:, :]
-    sent_ref[TURN:, :] = sent[:TURN, :]
-    hubs_ref[...] = picked(hub_ref)
+    sent = jnp.concatenate([sent[TURN:, :], sent[:TURN, :]], axis=0)
+    sent_ref[...] = sent.reshape(sent_ref.shape).astype(BF16)
+    hubs_ref[...] = picked(hub_ref).astype(BF16)
 
 
 def prep_kernel(
@@ -134,17 +134,22 @@
 
 
 def middle_kernel(
-    rem_ref, atrem_ref, bnd_ref, hub_ref, part_ref, self_ref, cot_ref, xt_ref, wn_ref, wnt_ref,
-    act_ref, pg_ref, ag_ref, bg_ref, load_ref,
+    rem_ref, atrem_ref, bnd_ref, hub0_ref, hub1_ref, hub2_ref, hub3_ref, part_ref, self_ref, cot_ref, xt_ref, wn_ref, wnt_ref,
+    act_ref, pg_ref, ag_ref, bg_ref, load_ref, hub_ref,
 ):
     scale = 1.0 / math.sqrt(1048576)
+    here = lax.axis_index("d") // 2 % 4
+    for bit, block_ref in enumerate((hub0_ref, hub1_ref, hub2_ref, hub3_ref)):
+        row = pl.multiple_of((here ^ bit) * 2 * HUB_DEV, 2 * HUB_DEV)
+        hub_ref[pl.ds(row, 2 * HUB_DEV), :] = block_ref[...]
+    bnd = bnd_ref[...].reshape(HALO, D)
     gself = jnp.zeros((D, D), F32)
     gnbr = jnp.zeros((D, D), F32)
     for i in range(ROWS // CHUNK):
         rows = slice(i * CHUNK, (i + 1) * CHUNK)
         agg = (
             part_ref[rows, :]
-            + dot(rem_ref[rows, :HALO], bnd_ref[...])
+            + dot(rem_ref[rows, :HALO], bnd)
             + dot(rem_ref[rows, HALO:], hub_ref[...])
         ).astype(BF16)
         pre = self_ref[rows, :] + dot(agg, wn_ref[...])
@@ -247,12 +252,13 @@
 ):
     mib = 1 << 20
     sent, hubs = call(
-        pick_kernel, [((HALO, D), BF16), ((HUB_DEV, D), BF16)], [VM] * 3, flops=1 << 28, nbytes=mib
+        pick_kernel, [((HALO // 2, 2, D), BF16), ((HUB_DEV, D), BF16)], [VM] * 3, flops=1 << 28, nbytes=mib
     )(send_rows, hub_rows, features)
     boundary = swap_rows(sent, (0, 1, 2), ZH // 2)
-    hub_copies = hubs
-    for axis in (4, 3):
-        hub_copies = lax.all_gather(hub_copies, "d", axis_index_groups=groups((axis,)), axis=0, tiled=True)
+    hubs = lax.all_gather(hubs, "d", axis_index_groups=groups((4,)), axis=0, tiled=True)
+    hub_blocks = [hubs]
+    for bit in (1, 2, 3):
+        hub_blocks.append(lax.ppermute(hubs, "d", [(i, i ^ (2 * bit)) for i in range(ALONG.size)]))
     rem, at_rem, part, self_pre, xt, wnt = call(
         prep_kernel,
         [
@@ -277,11 +283,12 @@
             ((HALO, D), BF16),
             ((8 * LOAD, HALF), F32),
         ],
-        [VM] * 10,
+        [VM] * 13,
+        scratch=[pltpu.VMEM((HUBS, D), BF16)],
         flops=1 << 30,
         nbytes=8 * mib,
         trans=1 << 19,
-    )(rem, at_rem, boundary, hub_copies, part, self_pre, cotangent, xt, w_nbr, wnt)
+    )(rem, at_rem, boundary, *hub_blocks, part, self_pre, cotangent, xt, w_nbr, wnt)
 
     load = swap_rows(load, (3, 4))
     near, hub_sums = call(

time: 158 us -> 154 us (0.975)
  blocking collectives: 78.7 us -> 66.2 us
  starting transfers between devices: 47.9 us -> 56.9 us
  Pallas kernels: 18.6 us -> 20.3 us
  local copies, waits for them, and re-layouts: 2.37 us -> 0.71 us
    all_gather x2 -> x1, blocking collectives: 13.6 us -> 2.94 us  [per_device(): lax.all_gather(hubs, 'd', axis_index_groups=groups((4,)), axis=0, tiled=T...]
    ppermute x0 -> x3, starting transfers between devices: none -> 8.97 us  [per_device(): lax.ppermute(hubs, 'd', [(i, i ^ 2 * bit) for i in range(ALONG.size)])]
    all_to_all x2 -> x0, local copies, waits for them, and re-layouts: 2.33 us -> none  [swap_rows(): lax.all_to_all(array, 'd', 0, 0, axis_index_groups=groups(order, turn), t...]
    all_to_all x3, blocking collectives: 65.1 us -> 63.2 us  [swap_rows(): lax.all_to_all(array, 'd', 0, 0, axis_index_groups=groups(order, turn), t...]
  transfers between devices with their start and end apart: 2 -> 5, of which waited for: 1 -> 1; matrix products, arithmetic and copies ran while one was open for 0% -> 0% of each run, Pallas kernels for 6% -> 8%
where the time goes in v3:
time: 154 us; the launch traced here: 153 us
  blocking collectives  66.2 us (43%)
  starting transfers between devices  56.9 us (37%)
  Pallas kernels  20.3 us (13%)
  waiting for transfers between devices  7.13 us (5%)
    all_to_all x3, blocking collectives, swap_rows(): lax.all_to_all(array, 'd', 0, 0, axis_index_groups=groups(order, turn), t...  63.2 us
    all_to_all x2, starting transfers between devices, swap_rows(): lax.all_to_all(array, 'd', 0, 0, axis_index_groups=groups(order, turn), t...  47.9 us
    ppermute x3, starting transfers between devices, per_device(): lax.ppermute(hubs, 'd', [(i, i ^ 2 * bit) for i in range(ALONG.size)])  8.97 us
    all_to_all x2, waiting for transfers between devices, swap_rows(): lax.all_to_all(array, 'd', 0, 0, axis_index_groups=groups(order, turn), t...  7.12 us
    pallas_call x1, Pallas kernels, per_device(): call(prep_kernel, [((ROWS, HALO + HUBS), BF16), ((HALO + HUBS, ROWS), BF1...  5.83 us
    pallas_call x1, Pallas kernels, per_device(): call(final_kernel, [((ROWS, D), BF16)], [SM] * 3 + [VM] * 8, scratch=[plt...  5.73 us
    pallas_call x1, Pallas kernels, per_device(): call(middle_kernel, [((ROWS, D), BF16), ((ROWS, D), BF16), ((ROWS, D), BF...  5.53 us
  transfers between devices with their start and end apart: 5, of which 1 were waited for; matrix products, arithmetic and copies ran while one was open for 0% of the time, Pallas kernels for 8%

profile of v3, /device:TPU:1, one launch (start us, length us, event | category | flops | bytes accessed | tf_op | source)
XLA Modules:
  0.0 153.5 jit_solution(1457295816012987696)
XLA Ops:
  0.6 2.2 %shard_map.130 = (bf16[128,2,256]{2,1,0:T(2,128)(2,1)}, bf16[16,256]{1,0:T(8,128)(2,1)}) custom-call(s32[1,256]{1,0:T(1,128)} %send_ref.3, s32[1,16]{1,0:T(1,128)} %hub_ref.3, bf16[1024,256]{1,0:T(8,128)(2,1)} %x_ref.3), custom_call_target="tpu_custom_call" | custom-call | flops 268435456 | bytes 1048576 | tf_op jit(solution)/shard_map/pallas_call | solution.py:254
  2.9 40.3 %all-to-all-start = ((bf16[128,2,256]{2,1,0:T(2,128)(2,1)}), bf16[128,2,256]{2,1,0:T(2,128)(2,1)S(1)}, u32[]{:S(2)}, u32[]{:S(2)}) async-start(bf16[128,2,256]{2,1,0:T(2,128)(2,1)} %get-tuple-element.21), calls=%async_computation | async-start | bytes 262144 | tf_op jit(solution)/shard_map/all_to_all | solution.py:42
  43.2 2.9 %all_gather.3.hub0_ref = bf16[32,256]{1,0:T(8,128)(2,1)S(1)} all-gather(bf16[16,256]{1,0:T(8,128)(2,1)} %get-tuple-element.22), channel_id=1, replica_groups={{0,1},{2,3},{4,5},{6,7},{8,9},{10,11},{12,13},{14,15},{16,17},{18,19},{..., dimensions={0}, use_global_device_ids=true | all-gather | bytes 24576 | tf_op jit(solution)/shard_map/all_gather | solution.py:258
  46.1 0.0 copy-start.4
  46.1 4.4 %collective-permute-start.2 = (bf16[32,256]{1,0:T(8,128)(2,1)S(1)}, bf16[32,256]{1,0:T(8,128)(2,1)S(1)}, u32[]{:S(2)}, u32[]{:S(2)}) collective-permute-start(bf16[32,256]{1,0:T(8,128)(2,1)S(1)} %all_gather.3.hub0_ref), channel_id=1, source_target_pairs={{0,6},{1,7},{2,4},{3,5},{4,2},{5,3},{6,0},{7,1},{8,14},{9,15},{10,... | collective-permute-start | bytes 49160 | tf_op jit(solution)/shard_map/ppermute | solution.py:261
  50.5 2.4 %collective-permute-start.1 = (bf16[32,256]{1,0:T(8,128)(2,1)S(1)}, bf16[32,256]{1,0:T(8,128)(2,1)S(1)}, u32[]{:S(2)}, u32[]{:S(2)}) collective-permute-start(bf16[32,256]{1,0:T(8,128)(2,1)S(1)} %all_gather.3.hub0_ref), channel_id=1, source_target_pairs={{0,4},{1,5},{2,6},{3,7},{4,0},{5,1},{6,2},{7,3},{8,12},{9,13},{10,... | collective-permute-start | bytes 49160 | tf_op jit(solution)/shard_map/ppermute | solution.py:261
  52.9 2.2 %collective-permute-start = (bf16[32,256]{1,0:T(8,128)(2,1)S(1)}, bf16[32,256]{1,0:T(8,128)(2,1)S(1)}, u32[]{:S(2)}, u32[]{:S(2)}) collective-permute-start(bf16[32,256]{1,0:T(8,128)(2,1)S(1)} %all_gather.3.hub0_ref), channel_id=1, source_target_pairs={{0,2},{1,3},{2,0},{3,1},{4,6},{5,7},{6,4},{7,5},{8,10},{9,11},{10,... | collective-permute-start | bytes 49160 | tf_op jit(solution)/shard_map/ppermute | solution.py:261
  55.7 5.8 %shard_map.129 = (bf16[1024,384]{1,0:T(8,128)(2,1)}, bf16[384,1024]{1,0:T(8,128)(2,1)}, f32[1024,256]{1,0:T(8,128)}, f32[1024,256]{1,0:T(8,128)}, bf16[256,1024]{1,0:T(8,128)(2,1)}, /*index=5*/bf16[256,256]{1,0:T(8,128)(2,1)}) custom-call(s32[1]{0:T(128)S(6)} %copy.14.count_ref, s32[1,40]{1,0:T(1,128)} %dst_ref.3, s32[1,40]{1,0:T(1,128)} %src_ref.3, ...), custom_call_target="tpu_custom_call" | custom-call | flops 1073741824 | bytes 9437184 | tf_op jit(solution)/shard_map/pallas_call | solution.py:262
  61.6 0.0 copy-done.4
  61.6 0.0 collective-permute-done.2.hub3_ref
  61.6 0.0 copy-start.5
  61.6 0.0 collective-permute-done.1.hub2_ref
  61.6 0.0 copy-start.6
  61.6 0.0 collective-permute-done.hub1_ref
  61.6 0.0 copy-start.7
  61.6 0.0 all-to-all-done.bnd_ref
  61.6 0.0 copy-start.3
  61.7 0.5 copy-done.5
  62.2 0.0 copy-done.6
  62.2 0.0 copy-done.7
  62.2 0.1 copy-done.3
  62.3 5.5 %shard_map.131 = (bf16[1024,256]{1,0:T(8,128)(2,1)}, bf16[1024,256]{1,0:T(8,128)(2,1)}, bf16[1024,256]{1,0:T(8,128)(2,1)}, bf16[256,256]{1,0:T(8,128)(2,1)}, f32[1280,128]{1,0:T(8,128)}) custom-call(bf16[1024,384]{1,0:T(8,128)(2,1)} %get-tuple-element.19.rem_ref, bf16[384,1024]{1,0:T(8,128)(2,1)} %get-tuple-element.20.atrem_ref, ...), custom_call_target="tpu_custom_call" | custom-call | flops 1073741824 | bytes 8388608 | tf_op jit(solution)/shard_map/pallas_call | solution.py:277
  67.8 0.0 copy-start.1
  67.8 16.2 %all_to_all.47 = f32[8,160,128]{2,1,0:T(8,128)S(1)} all-to-all(f32[8,160,128]{2,1,0:T(8,128)} %bitcast.21), channel_id=1, replica_groups={{0,1,2,3,4,5,6,7},{8,9,10,11,12,13,14,15},{16,17,18,19,20,21,22,23},{24..., dimensions={0} | all-to-all | bytes 1310720 | tf_op jit(solution)/shard_map/all_to_all | solution.py:42
  84.0 0.0 copy-done.1
  84.1 0.0 copy-start.2
  84.1 12.2 %all_to_all.48 = bf16[16,16,384]{2,1,0:T(8,128)(2,1)S(1)} all-to-all(bf16[16,16,384]{2,1,0:T(8,128)(2,1)S(1)} %bitcast.18), channel_id=1, replica_groups={{0,8,16,24,32,40,48,56,64,72,80,88,96,104,112,120},{1,9,17,25,33,41,49,..., dimensions={0} | all-to-all | bytes 393216 | tf_op jit(solution)/shard_map/all_to_all | solution.py:42
  96.3 0.2 shard_map.133
  96.5 34.9 %all_to_all.49 = bf16[8,40,256]{2,1,0:T(8,128)(2,1)S(1)} all-to-all(bf16[8,40,256]{2,1,0:T(8,128)(2,1)S(1)} %bitcast.17), channel_id=1, replica_groups={{512,640,768,896,0,128,256,384},{513,641,769,897,1,129,257,385},{514,64..., dimensions={0} | all-to-all | bytes 327680 | tf_op jit(solution)/shard_map/all_to_all | solution.py:42
  131.4 0.0 copy-done.2
  131.4 0.0 copy-start
  131.4 0.8 shard_map.135
  132.1 7.6 %all-to-all-start.4 = ((bf16[128,8,128]{2,1,0:T(8,128)(2,1)}), bf16[128,8,128]{2,1,0:T(8,128)(2,1)S(1)}, u32[]{:S(2)}, u32[]{:S(2)}) async-start(bf16[128,8,128]{2,1,0:T(8,128)(2,1)} %bitcast.6), calls=%async_computation.4 | async-start | bytes 524288 | tf_op jit(solution)/shard_map/all_to_all | solution.py:42
  139.7 0.0 copy-done
  139.8 5.7 %shard_map.134 = bf16[1024,256]{1,0:T(8,128)(2,1)} custom-call(s32[1]{0:T(128)S(6)} %copy.14.count_ref, s32[1,40]{1,0:T(1,128)} %dst_ref.3, s32[1,40]{1,0:T(1,128)} %src_ref.3, s32[1,256]{1,0:T(1,128)} %send_ref.3, s32[1,16]{1,0:T(1,128)} %hub_ref.3, bf16[320,256]{1,0:T(8,128)(2,1)} %bitcast.16, f32[16,256]{1,0:T(8,128)} %copy-done.2, ...), custom_call_target="tpu_custom_call" | custom-call | flops 1073741824 | bytes 5242880 | tf_op jit(solution)/shard_map/pallas_call | solution.py:302
  145.5 7.1 %all-to-all-done.4 = bf16[128,8,128]{2,1,0:T(8,128)(2,1)S(1)} async-done(((bf16[128,8,128]{2,1,0:T(8,128)(2,1)}), bf16[128,8,128]{2,1,0:T(8,128)(2,1)S(1)}, u32[]{:S(2)}, u32[]{:S(2)}) %all-to-all-start.4) | async-done | bytes 262176 | tf_op jit(solution)/shard_map/all_to_all | solution.py:42
  152.6 0.8 fusion.2
  (2 shorter events, 0.1 us)
Async XLA Ops:
  2.9 58.8 %all-to-all-start = ((bf16[128,2,256]{2,1,0:T(2,128)(2,1)}), bf16[128,2,256]{2,1,0:T(2,128)(2,1)S(1)}, u32[]{:S(2)}, u32[]{:S(2)}) async-start(bf16[128,2,256]{2,1,0:T(2,128)(2,1)} %get-tuple-element.21), calls=%async_computation | async-start | bytes 262144 | tf_op jit(solution)/shard_map/all_to_all | solution.py:42
  46.1 15.5 %copy-start.4 = (bf16[32,256]{1,0:T(8,128)(2,1)}, bf16[32,256]{1,0:T(8,128)(2,1)S(1)}, u32[]{:S(2)}) copy-start(bf16[32,256]{1,0:T(8,128)(2,1)S(1)} %all_gather.3.hub0_ref) | copy-start | bytes 49156
  46.1 15.5 %collective-permute-start.2 = (bf16[32,256]{1,0:T(8,128)(2,1)S(1)}, bf16[32,256]{1,0:T(8,128)(2,1)S(1)}, u32[]{:S(2)}, u32[]{:S(2)}) collective-permute-start(bf16[32,256]{1,0:T(8,128)(2,1)S(1)} %all_gather.3.hub0_ref), channel_id=1, source_target_pairs={{0,6},{1,7},{2,4},{3,5},{4,2},{5,3},{6,0},{7,1},{8,14},{9,15},{10,... | collective-permute-start | bytes 49160 | tf_op jit(solution)/shard_map/ppermute | solution.py:261
  50.5 11.1 %collective-permute-start.1 = (bf16[32,256]{1,0:T(8,128)(2,1)S(1)}, bf16[32,256]{1,0:T(8,128)(2,1)S(1)}, u32[]{:S(2)}, u32[]{:S(2)}) collective-permute-start(bf16[32,256]{1,0:T(8,128)(2,1)S(1)} %all_gather.3.hub0_ref), channel_id=1, source_target_pairs={{0,4},{1,5},{2,6},{3,7},{4,0},{5,1},{6,2},{7,3},{8,12},{9,13},{10,... | collective-permute-start | bytes 49160 | tf_op jit(solution)/shard_map/ppermute | solution.py:261
  52.9 8.7 %collective-permute-start = (bf16[32,256]{1,0:T(8,128)(2,1)S(1)}, bf16[32,256]{1,0:T(8,128)(2,1)S(1)}, u32[]{:S(2)}, u32[]{:S(2)}) collective-permute-start(bf16[32,256]{1,0:T(8,128)(2,1)S(1)} %all_gather.3.hub0_ref), channel_id=1, source_target_pairs={{0,2},{1,3},{2,0},{3,1},{4,6},{5,7},{6,4},{7,5},{8,10},{9,11},{10,... | collective-permute-start | bytes 49160 | tf_op jit(solution)/shard_map/ppermute | solution.py:261
  61.6 0.6 copy-start.5
  61.6 0.6 copy-start.6
  61.6 0.6 copy-start.7
  61.6 0.7 copy-start.3
  67.8 16.2 %copy-start.1 = (bf16[256,256]{1,0:T(8,128)(2,1)S(1)}, bf16[256,256]{1,0:T(8,128)(2,1)}, u32[]{:S(2)}) copy-start(bf16[256,256]{1,0:T(8,128)(2,1)} %get-tuple-element.29.bg_ref) | copy-start | bytes 393220
  84.1 47.3 %copy-start.2 = (f32[16,256]{1,0:T(8,128)}, f32[16,256]{1,0:T(8,128)S(1)}, u32[]{:S(2)}) copy-start(f32[16,256]{1,0:T(8,128)S(1)} %get-tuple-element.31.hsum_ref) | copy-start | bytes 49156
  131.4 8.4 %copy-start = (bf16[8,40,256]{2,1,0:T(8,128)(2,1)}, bf16[8,40,256]{2,1,0:T(8,128)(2,1)S(1)}, u32[]{:S(2)}) copy-start(bf16[8,40,256]{2,1,0:T(8,128)(2,1)S(1)} %all_to_all.49) | copy-start | bytes 491524
  132.1 20.5 %all-to-all-start.4 = ((bf16[128,8,128]{2,1,0:T(8,128)(2,1)}), bf16[128,8,128]{2,1,0:T(8,128)(2,1)S(1)}, u32[]{:S(2)}, u32[]{:S(2)}) async-start(bf16[128,8,128]{2,1,0:T(8,128)(2,1)} %bitcast.6), calls=%async_computation.4 | async-start | bytes 524288 | tf_op jit(solution)/shard_map/all_to_all | solution.py:42
